TPU v7x, 32 devices: a whole 2x2x4 slice. The times are simulated.
32 devices in a mesh: grp: 2 (over y), srv: 16 (over z, x, core).
Axes of the slice: x: 2, y: 2, z: 4, core: 2. Of those that a mesh axis runs over, the one named last changes fastest.
Arguments:
- queries: bfloat16 [12288, 1536], P(('grp', 'srv')), parts along dimension 0, may hold values from -4096 to 4096
- latent_rope: bfloat16 [12288, 576], P(('grp', 'srv')), parts along dimension 0, may hold values from -16 to 16
- doc_start: int32 [12288], P(('grp', 'srv')), parts along dimension 0, may hold values from 0 to 6143, as said below
- w_kv_up: bfloat16 [512, 2048], replicated, may hold values from -0.25 to 0.25
- w_out: bfloat16 [1024, 2048], replicated, may hold values from -0.5 to 0.5
Outputs:
- mixed: bfloat16 [12288, 2048], P(('grp', 'srv')), parts along dimension 0
There are 2 independent parts, one for each index of `grp`. A program takes and returns all parts, laid end to end along the dimension named above; an argument that names none is the same for every part. Nothing has to cross between parts.
Inputs may be any that keep to these rules, and one draw needn't show every extreme that they name: doc_start[i] <= i < doc_start[i] + 2688; doc_start[i] is i or doc_start[i-1]; the first document has exactly 2688 positions.
All inputs are finite; a program needn't handle non-finite values.
Results may differ from a plain program's by a relative error of at most 0.0063.
Values may be sent and summed in bfloat16 or wider, within the bound.
A program may use at most 128 MiB of HBM per device.

v0:
```python
import math

import jax
import jax.numpy as jnp
from jax import lax
from jax.sharding import PartitionSpec as P

DN = 128
DR = 64
DV = 128
R = 512
REACH = 7


def passed_along(value, axis, steps):
    count = lax.axis_size(axis)
    initial, last = (max(0, -steps), min(count, count - steps))
    return lax.ppermute(value, axis, [(source, source + steps) for source in range(initial, last)])


def expand_rows(latent_part, w_kv_up, head_count):
    row_count = latent_part.shape[0]
    product = jnp.dot(latent_part, w_kv_up, preferred_element_type=jnp.float32)
    return product.astype(jnp.bfloat16).reshape(row_count, head_count, -1)


def block_terms(query_nope, query_rope, key_nope, values, key_rope, query_pos, key_pos, starts):
    score_scale = 1.0 / math.sqrt(query_nope.shape[-1] + query_rope.shape[-1])
    scores = jnp.einsum("ihc,jhc->hij", query_nope, key_nope, preferred_element_type=jnp.float32)
    scores = scores + jnp.einsum(
        "ihc,jc->hij", query_rope, key_rope, preferred_element_type=jnp.float32
    )
    scores = scores * score_scale
    allowed = (key_pos[None, :] >= starts[:, None]) & (key_pos[None, :] <= query_pos[:, None])
    masked = jnp.where(allowed[None], scores, -jnp.inf)
    block_max = jnp.maximum(jnp.max(masked, axis=2), jnp.float32(-1e30))
    weights = jnp.where(allowed[None], jnp.exp(scores - block_max[:, :, None]), jnp.float32(0.0))
    block_total = jnp.sum(weights, axis=2)
    block_out = jnp.einsum(
        "hij,jhc->ihc", weights.astype(jnp.bfloat16), values, preferred_element_type=jnp.float32
    )
    return (block_out, block_max, block_total)


def merge_blocks(pieces):
    top_max = pieces[0][1]
    for block_part in pieces[1:]:
        top_max = jnp.maximum(top_max, block_part[1])
    numerator = jnp.zeros(pieces[0][0].shape, jnp.float32)
    denominator = jnp.zeros(pieces[0][0].shape[:2] + (1,), jnp.float32)
    for block_part in pieces:
        factor = jnp.exp(block_part[1] - top_max)
        numerator = numerator + factor.T[:, :, None] * block_part[0]
        denominator = denominator + (factor * block_part[2]).T[:, :, None]
    return (numerator / denominator).astype(jnp.bfloat16)


def local(queries, latent_rope, doc_start, w_kv_up, w_out):
    row_count = queries.shape[0]
    head_count = w_out.shape[0] // DV
    query_all = queries.reshape(row_count, head_count, DN + DR)
    query_nope = query_all[:, :, :DN]
    query_rope = query_all[:, :, DN:]
    device_slot = lax.axis_index("srv")
    query_pos = device_slot * row_count + jnp.arange(row_count, dtype=jnp.int32)
    own_kv = expand_rows(latent_rope[:, :R], w_kv_up, head_count)
    own_rope = latent_rope[:, R:]
    pieces = [
        block_terms(
            query_nope,
            query_rope,
            own_kv[:, :, :DN],
            own_kv[:, :, DN:],
            own_rope,
            query_pos,
            query_pos,
            doc_start,
        )
    ]
    for distance in range(1, REACH + 1):
        key_kv, key_rope = passed_along((own_kv, own_rope), "srv", distance)
        key_pos = query_pos - distance * row_count
        pieces.append(
            block_terms(
                query_nope,
                query_rope,
                key_kv[:, :, :DN],
                key_kv[:, :, DN:],
                key_rope,
                query_pos,
                key_pos,
                doc_start,
            )
        )
    attended = merge_blocks(pieces).reshape(row_count, head_count * DV)
    return jnp.dot(attended, w_out, preferred_element_type=jnp.float32).astype(jnp.bfloat16)


def solution(mesh):
    in_specs = (P(("grp", "srv"), None), P(("grp", "srv"), None), P(("grp", "srv")), P(), P())
    out_specs = P(("grp", "srv"), None)
    return jax.shard_map(local, mesh=mesh, in_specs=in_specs, out_specs=out_specs, check_vma=False)
```

profile of v0, /device:TPU:25, one launch (start us, length us, event | category | flops | bytes accessed | tf_op | source)
XLA Modules:
  0.0 362.1 jit_solution(5786521444005505611)
XLA Ops:
  0.0 1.6 copy-done
  1.6 2.0 convolution_convert_fusion.1
  10.0 3.1 collective-permute-start.2
  13.2 1.9 collective-permute-start
  15.9 1.9 fusion.96
  19.0 2.1 select_reduce_fusion.7
  25.0 71.7 %collective-permute-done = bf16[384,8,256]{2,0,1:T(8,128)(2,1)} collective-permute-done((bf16[384,8,256]{2,0,1:T(8,128)(2,1)}, bf16[384,8,256]{2,0,1:T(8,128)(2,1)}, u32[]{:S(2)}, u32[]{:S(2)}) %collective-permute-start) | collective-permute-done | bytes 1572896 | tf_op jit(solution)/shard_map/ppermute | solution.py:18
  97.9 1.9 fusion.94
  99.8 31.4 %collective-permute-done.2 = bf16[384,8,256]{2,0,1:T(8,128)(2,1)} collective-permute-done((bf16[384,8,256]{2,0,1:T(8,128)(2,1)}, bf16[384,8,256]{2,0,1:T(8,128)(2,1)}, u32[]{:S(2)}, u32[]{:S(2)}) %collective-permute-start.2) | collective-permute-done | bytes 1572896 | tf_op jit(solution)/shard_map/ppermute | solution.py:18
  132.5 1.9 fusion.92
  135.7 1.9 fusion.90
  138.9 1.9 fusion.88
  142.1 1.9 fusion.86
  144.0 156.8 %collective-permute-done.10 = bf16[384,8,256]{2,0,1:T(8,128)(2,1)S(1)} collective-permute-done((bf16[384,8,256]{2,0,1:T(8,128)(2,1)}, bf16[384,8,256]{2,0,1:T(8,128)(2,1)S(1)}, u32[]{:S(2)}, u32[]{:S(2)}) %collective-permute-start.10) | collective-permute-done | bytes 1572896 | tf_op jit(solution)/shard_map/ppermute | solution.py:18
  302.9 19.0 %collective-permute-start.1 = (bf16[384,64]{0,1:T(8,128)(2,1)S(1)}, bf16[384,64]{0,1:T(8,128)(2,1)S(1)}, u32[]{:S(2)}, u32[]{:S(2)}) collective-permute-start(bf16[384,64]{0,1:T(8,128)(2,1)S(1)} %slice.63), channel_id=1, source_target_pairs={{0,1},{1,2},{2,3},{3,4},{4,5},{5,6},{6,7},{7,8},{8,9},{9,10},{10,1... | collective-permute-start | bytes 147464 | tf_op jit(solution)/shard_map/ppermute | solution.py:18
  323.1 1.9 collective-permute-start.3
  326.2 2.6 collective-permute-done.3
  344.0 2.4 fusion.36
  346.5 2.2 fusion.34
  348.7 2.2 fusion.32
  350.9 2.2 fusion.30
  353.1 2.3 fusion.28
  356.9 2.2 fusion.66
  359.1 3.0 convolution_convert_fusion
  (109 shorter events, 39.3 us)
Async XLA Ops:
  0.0 15.1 %copy-start.8 = (bf16[384,1536]{1,0:T(8,128)(2,1)S(1)}, bf16[384,1536]{1,0:T(8,128)(2,1)}, u32[]{:S(2)}) copy-start(bf16[384,1536]{1,0:T(8,128)(2,1)} %param.5) | copy-start | bytes 3538948
  6.0 11.8 %copy-start.24 = (s32[384]{0:T(512)S(1)}, s32[384]{0:T(512)}, u32[]{:S(2)}) copy-start(s32[384]{0:T(512)} %param.7) | copy-start | bytes 4612
  6.0 134.8 %collective-permute-start.8 = (bf16[384,8,256]{2,0,1:T(8,128)(2,1)}, bf16[384,8,256]{2,0,1:T(8,128)(2,1)}, u32[]{:S(2)}, u32[]{:S(2)}) collective-permute-start(bf16[384,8,256]{2,0,1:T(8,128)(2,1)} %bitcast.250), channel_id=1, source_target_pairs={{0,5},{1,6},{2,7},{3,8},{4,9},{5,10},{6,11},{7,12},{8,13},{9,14},{... | collective-permute-start | bytes 4718600 | tf_op jit(solution)/shard_map/ppermute | solution.py:18
  7.4 130.2 %collective-permute-start.6 = (bf16[384,8,256]{2,0,1:T(8,128)(2,1)}, bf16[384,8,256]{2,0,1:T(8,128)(2,1)}, u32[]{:S(2)}, u32[]{:S(2)}) collective-permute-start(bf16[384,8,256]{2,0,1:T(8,128)(2,1)} %bitcast.250), channel_id=1, source_target_pairs={{0,4},{1,5},{2,6},{3,7},{4,8},{5,9},{6,10},{7,11},{8,12},{9,13},{1... | collective-permute-start | bytes 4718600 | tf_op jit(solution)/shard_map/ppermute | solution.py:18
  8.7 125.7 %collective-permute-start.4 = (bf16[384,8,256]{2,0,1:T(8,128)(2,1)}, bf16[384,8,256]{2,0,1:T(8,128)(2,1)}, u32[]{:S(2)}, u32[]{:S(2)}) collective-permute-start(bf16[384,8,256]{2,0,1:T(8,128)(2,1)} %bitcast.250), channel_id=1, source_target_pairs={{0,3},{1,4},{2,5},{3,6},{4,7},{5,8},{6,9},{7,10},{8,11},{9,12},{10... | collective-permute-start | bytes 4718600 | tf_op jit(solution)/shard_map/ppermute | solution.py:18
  10.0 121.2 %collective-permute-start.2 = (bf16[384,8,256]{2,0,1:T(8,128)(2,1)}, bf16[384,8,256]{2,0,1:T(8,128)(2,1)}, u32[]{:S(2)}, u32[]{:S(2)}) collective-permute-start(bf16[384,8,256]{2,0,1:T(8,128)(2,1)} %bitcast.250), channel_id=1, source_target_pairs={{0,2},{1,3},{2,4},{3,5},{4,6},{5,7},{6,8},{7,9},{8,10},{9,11},{10,... | collective-permute-start | bytes 4718600 | tf_op jit(solution)/shard_map/ppermute | solution.py:18
  13.2 83.5 %collective-permute-start = (bf16[384,8,256]{2,0,1:T(8,128)(2,1)}, bf16[384,8,256]{2,0,1:T(8,128)(2,1)}, u32[]{:S(2)}, u32[]{:S(2)}) collective-permute-start(bf16[384,8,256]{2,0,1:T(8,128)(2,1)} %bitcast.250), channel_id=1, source_target_pairs={{0,1},{1,2},{2,3},{3,4},{4,5},{5,6},{6,7},{7,8},{8,9},{9,10},{10,1... | collective-permute-start | bytes 4718600 | tf_op jit(solution)/shard_map/ppermute | solution.py:18
  19.0 2.1 copy-start.3
  96.6 204.2 %collective-permute-start.10 = (bf16[384,8,256]{2,0,1:T(8,128)(2,1)}, bf16[384,8,256]{2,0,1:T(8,128)(2,1)S(1)}, u32[]{:S(2)}, u32[]{:S(2)}) collective-permute-start(bf16[384,8,256]{2,0,1:T(8,128)(2,1)} %bitcast.250), channel_id=1, source_target_pairs={{0,6},{1,7},{2,8},{3,9},{4,10},{5,11},{6,12},{7,13},{8,14},{9,15},... | collective-permute-start | bytes 4718600 | tf_op jit(solution)/shard_map/ppermute | solution.py:18
  131.2 171.7 %collective-permute-start.12 = (bf16[384,8,256]{2,0,1:T(8,128)(2,1)}, bf16[384,8,256]{2,0,1:T(8,128)(2,1)S(1)}, u32[]{:S(2)}, u32[]{:S(2)}) collective-permute-start(bf16[384,8,256]{2,0,1:T(8,128)(2,1)} %bitcast.250), channel_id=1, source_target_pairs={{0,7},{1,8},{2,9},{3,10},{4,11},{5,12},{6,13},{7,14},{8,15},{16,23... | collective-permute-start | bytes 4718600 | tf_op jit(solution)/shard_map/ppermute | solution.py:18
  134.4 200.6 %collective-permute-start.11 = (bf16[384,64]{0,1:T(8,128)(2,1)S(1)}, bf16[384,64]{0,1:T(8,128)(2,1)S(1)}, u32[]{:S(2)}, u32[]{:S(2)}) collective-permute-start(bf16[384,64]{0,1:T(8,128)(2,1)S(1)} %slice.63), channel_id=1, source_target_pairs={{0,6},{1,7},{2,8},{3,9},{4,10},{5,11},{6,12},{7,13},{8,14},{9,15},... | collective-permute-start | bytes 147464 | tf_op jit(solution)/shard_map/ppermute | solution.py:18
  137.6 196.2 %collective-permute-start.9 = (bf16[384,64]{0,1:T(8,128)(2,1)S(1)}, bf16[384,64]{0,1:T(8,128)(2,1)S(1)}, u32[]{:S(2)}, u32[]{:S(2)}) collective-permute-start(bf16[384,64]{0,1:T(8,128)(2,1)S(1)} %slice.63), channel_id=1, source_target_pairs={{0,5},{1,6},{2,7},{3,8},{4,9},{5,10},{6,11},{7,12},{8,13},{9,14},{... | collective-permute-start | bytes 147464 | tf_op jit(solution)/shard_map/ppermute | solution.py:18
  140.8 191.8 %collective-permute-start.7 = (bf16[384,64]{0,1:T(8,128)(2,1)S(1)}, bf16[384,64]{0,1:T(8,128)(2,1)S(1)}, u32[]{:S(2)}, u32[]{:S(2)}) collective-permute-start(bf16[384,64]{0,1:T(8,128)(2,1)S(1)} %slice.63), channel_id=1, source_target_pairs={{0,4},{1,5},{2,6},{3,7},{4,8},{5,9},{6,10},{7,11},{8,12},{9,13},{1... | collective-permute-start | bytes 147464 | tf_op jit(solution)/shard_map/ppermute | solution.py:18
  300.8 2.1 copy-start.6
  300.8 30.6 %collective-permute-start.5 = (bf16[384,64]{0,1:T(8,128)(2,1)S(1)}, bf16[384,64]{0,1:T(8,128)(2,1)S(1)}, u32[]{:S(2)}, u32[]{:S(2)}) collective-permute-start(bf16[384,64]{0,1:T(8,128)(2,1)S(1)} %slice.63), channel_id=1, source_target_pairs={{0,3},{1,4},{2,5},{3,6},{4,7},{5,8},{6,9},{7,10},{8,11},{9,12},{10... | collective-permute-start | bytes 147464 | tf_op jit(solution)/shard_map/ppermute | solution.py:18
  302.9 22.1 %copy-start.4 = (bf16[384,8,256]{2,0,1:T(8,128)(2,1)}, bf16[384,8,256]{2,0,1:T(8,128)(2,1)S(1)}, u32[]{:S(2)}) copy-start(bf16[384,8,256]{2,0,1:T(8,128)(2,1)S(1)} %collective-permute-done.12) | copy-start | bytes 4718596
  302.9 20.2 %collective-permute-start.1 = (bf16[384,64]{0,1:T(8,128)(2,1)S(1)}, bf16[384,64]{0,1:T(8,128)(2,1)S(1)}, u32[]{:S(2)}, u32[]{:S(2)}) collective-permute-start(bf16[384,64]{0,1:T(8,128)(2,1)S(1)} %slice.63), channel_id=1, source_target_pairs={{0,1},{1,2},{2,3},{3,4},{4,5},{5,6},{6,7},{7,8},{8,9},{9,10},{10,1... | collective-permute-start | bytes 147464 | tf_op jit(solution)/shard_map/ppermute | solution.py:18
  323.1 5.7 %collective-permute-start.3 = (bf16[384,64]{0,1:T(8,128)(2,1)S(1)}, bf16[384,64]{0,1:T(8,128)(2,1)S(1)}, u32[]{:S(2)}, u32[]{:S(2)}) collective-permute-start(bf16[384,64]{0,1:T(8,128)(2,1)S(1)} %slice.63), channel_id=1, source_target_pairs={{0,2},{1,3},{2,4},{3,5},{4,6},{5,7},{6,8},{7,9},{8,10},{9,11},{10,... | collective-permute-start | bytes 147464 | tf_op jit(solution)/shard_map/ppermute | solution.py:18
  326.2 5.3 %copy-start.9 = (f32[8,384]{1,0:T(8,128)}, f32[8,384]{1,0:T(8,128)S(1)}, u32[]{:S(2)}) copy-start(f32[8,384]{1,0:T(8,128)S(1)} %get-tuple-element.32) | copy-start | bytes 36868
  328.8 7.4 %collective-permute-start.13 = (bf16[384,64]{0,1:T(8,128)(2,1)S(1)}, bf16[384,64]{0,1:T(8,128)(2,1)S(1)}, u32[]{:S(2)}, u32[]{:S(2)}) collective-permute-start(bf16[384,64]{0,1:T(8,128)(2,1)S(1)} %slice.63), channel_id=1, source_target_pairs={{0,7},{1,8},{2,9},{3,10},{4,11},{5,12},{6,13},{7,14},{8,15},{16,23... | collective-permute-start | bytes 147464 | tf_op jit(solution)/shard_map/ppermute | solution.py:18
  342.2 1.7 copy-start.10
  353.1 2.3 copy-start.7
  356.9 2.2 copy-start.25
  359.1 3.0 copy-start.1
  (16 other events, 22.9 us)
where the time goes:
time: 368 us; the launch traced here: 362 us
  waiting for transfers between devices  263 us (71%)
  matrix products  43.6 us (12%)
  starting transfers between devices  39.2 us (11%)
  other arithmetic  8.55 us (2%)
  local copies, waits for them, and re-layouts  7.07 us (2%)
    ppermute x14, waiting for transfers between devices, passed_along(): lax.ppermute(value, axis, [(source, source + steps) for source in range(i...  263 us
    ppermute x14, starting transfers between devices, passed_along(): lax.ppermute(value, axis, [(source, source + steps) for source in range(i...  39.2 us
    dot_general x8, matrix products, block_terms(): jnp.einsum('hij,jhc->ihc', weights.astype(jnp.bfloat16), values, preferre...  15.7 us
    dot_general x8, matrix products, block_terms(): jnp.einsum('ihc,jhc->hij', query_nope, key_nope, preferred_element_type=j...  12.9 us
    dot_general x8, matrix products, block_terms(): jnp.einsum('ihc,jc->hij', query_rope, key_rope, preferred_element_type=jn...  10 us
  transfers between devices with their start and end apart: 14, of which 5 were waited for; matrix products, arithmetic and copies ran while one was open for 8% of the time, Pallas kernels for 0%

commit v1 on v0

v1 whole, which is shorter than its diff:
```python
import functools
import math

import jax
import jax.numpy as jnp
from jax import lax
from jax.experimental import pallas as pl
from jax.experimental.pallas import tpu as pltpu
from jax.sharding import PartitionSpec as P

DN = 128
DR = 64
DV = 128
R = 512
REACH = 7
DQ = DN + DR
PARTS = 3
NEG = -1e30
MESH = pl.DeviceIdType.MESH

ORDER = ((4, 3, 7, 2, 1, 5, 6), (1, 4, 5, 2, 3, 6, 7), (2, 1, 4, 3, 7, 6, 5), (1, 2, 3, 4, 5, 6, 7))
TAKE = (
    ((4,), (3,), (7,), (2,), (1,), (5,), (6,)),
    ((1,), (4,), (5,), (2,), (3,), (6,), (7,)),
    ((2, 4), (1,), (), (3, 7), (6,), (), (5,)),
    ((1,), (2, 4), (3,), (), (6, 5), (), (7,)),
)


def kernel(n, heads, q_hbm, lat_hbm, start_hbm, wkv_hbm, wout_hbm, o_hbm,
           held, q_in, q_s, lat_in, start_in, start_s, wkv, wout, rope, acc, top, att, out,
           in_sem, out_sem, send_sem, recv_sem):
    rows = q_in.shape[0]
    part = rows // PARTS
    extra = part * DR // R
    me = lax.axis_index("srv")
    z, x, c = me // 4, (me // 2) % 2, me % 2
    depth = n // 4
    place = 2 * x + c
    scale = math.log2(math.e) / math.sqrt(DQ)

    loads = [
        pltpu.make_async_copy(a, b, in_sem.at[i])
        for i, (a, b) in enumerate(
            ((lat_hbm, lat_in), (q_hbm, q_in), (start_hbm, start_in), (wkv_hbm, wkv), (wout_hbm, wout))
        )
    ]
    for load in loads:
        load.start()

    has_next = z + 1 < depth
    middle = jnp.logical_and(z >= 1, has_next)
    partners = (
        (1 - 2 * c, True),
        (2 - 4 * x, True),
        (4, has_next),
        (-4, z >= 1),
        (3, jnp.logical_and(c == 1, middle)),
        (-3, jnp.logical_and(c == 0, z >= 2)),
    )
    barrier = pltpu.get_barrier_semaphore()
    for delta, cond in partners:
        def greet(delta=delta):
            pl.semaphore_signal(barrier, inc=1, device_id={"srv": me + delta}, device_id_type=MESH)
        greet() if cond is True else pl.when(cond)(greet)

    corner = jnp.logical_and(x == 0, c == 0)
    sends = (
        (0, 1, c == 0),
        (0, 2, x == 0),
        (0, 4, has_next),
        (2, 1 - 2 * c, me >= 2),
        (2, 4, jnp.logical_and(corner, middle)),
        (4, 1 - 2 * c, z >= 1),
        (4, 2 - 4 * x, z >= 1),
        (4, 3, jnp.logical_and(c == 1, middle)),
        (5, 1, jnp.logical_and(corner, z >= 2)),
        (6, 1 - 2 * c, jnp.logical_and(me >= 6, jnp.logical_or(x == 1, c == 0))),
        (7, -2, jnp.logical_and(jnp.logical_and(x == 1, c == 0), me >= 7)),
    )

    def remote(i, k):
        d, delta, _ = sends[i]
        return pltpu.make_async_remote_copy(
            src_ref=held.at[d, k],
            dst_ref=held.at[d + delta, k],
            send_sem=send_sem.at[i, k],
            recv_sem=recv_sem.at[d + delta, k],
            device_id={"srv": me + delta},
            device_id_type=MESH,
        )

    def pass_on(d, k):
        for i, (source, _, cond) in enumerate(sends):
            if source == d:
                pl.when(cond)(lambda i=i: remote(i, k).start())

    def take(distances):
        for k in range(PARTS):
            for d in distances:
                @pl.when(d <= me)
                def _(d=d):
                    pltpu.make_async_remote_copy(
                        src_ref=held.at[d, k],
                        dst_ref=held.at[d, k],
                        send_sem=send_sem.at[0, k],
                        recv_sem=recv_sem.at[d, k],
                        device_id={"srv": me + 1 - 2 * c},
                        device_id_type=MESH,
                    ).wait_recv()
                    pass_on(d, k)

    count = 2 + has_next.astype(jnp.int32) + (z >= 1).astype(jnp.int32)
    count = count + jnp.logical_and(c == 1, middle).astype(jnp.int32)
    count = count + jnp.logical_and(c == 0, z >= 2).astype(jnp.int32)

    loads[0].wait()
    for k in range(PARTS):
        held[0, k, :part, :] = lat_in[k * part:(k + 1) * part, :R]
        held[0, k, part:, :] = jnp.concatenate(
            [lat_in[k * part + g * extra:k * part + (g + 1) * extra, R:] for g in range(R // DR)], axis=1
        )
    pl.semaphore_wait(barrier, count)
    for k in range(PARTS):
        pass_on(0, k)

    loads[1].wait()
    for h in range(heads):
        q_s[h] = q_in[:, h * DQ:(h + 1) * DQ]
    loads[2].wait()
    starts = jnp.broadcast_to(start_in[...].astype(jnp.float32), (128, rows))
    start_s[...] = jnp.transpose(starts).astype(jnp.int32)
    loads[3].wait()

    def block(d, own):
        for k in range(PARTS):
            for g in range(R // DR):
                rope[k * part + g * extra:k * part + (g + 1) * extra, :] = held[
                    d, k, part:, g * DR:(g + 1) * DR
                ]
        first = start_s[...] - (me - d) * rows
        first = jnp.concatenate([first] * (rows // 128), axis=1)
        ones = jnp.ones((rows, 128), jnp.bfloat16)

        def one(h):
            latent = held[d, :, :part, :].reshape(rows, R)
            columns = pl.ds(pl.multiple_of(h * (DN + DV), DN + DV), DN + DV)
            kv = jnp.dot(latent, wkv[:, columns], preferred_element_type=jnp.float32).astype(jnp.bfloat16)
            keys = jnp.concatenate([kv[:, :DN], rope[...]], axis=1)
            values = jnp.concatenate([kv[:, DN:], ones], axis=1)
            s = lax.dot_general(
                q_s[h], keys, (((1,), (1,)), ((), ())), preferred_element_type=jnp.float32
            )
            position = lax.broadcasted_iota(jnp.int32, (rows, rows), 1)
            allowed = position >= first
            if own:
                row = lax.broadcasted_iota(jnp.int32, (rows, rows), 0)
                allowed = jnp.logical_and(allowed, position <= row)
            s = jnp.where(allowed, s, NEG)
            best = jnp.max(s, axis=1, keepdims=True)
            if own:
                new = jnp.broadcast_to(best, (rows, 128))
            else:
                old = top[h]
                new = jnp.maximum(old, best)
            p = jnp.exp2((s - jnp.concatenate([new] * (rows // 128), axis=1)) * scale)
            pv = jnp.dot(p.astype(jnp.bfloat16), values, preferred_element_type=jnp.float32)
            if own:
                acc[h] = pv
            else:
                factor = jnp.exp2((old - new) * scale)
                acc[h] = acc[h] * jnp.concatenate([factor, factor], axis=1) + pv
            top[h] = new

        @pl.loop(0, heads // 2)
        def _(pair):
            one(2 * pair)
            one(2 * pair + 1)

    block(0, True)

    def digits(order):
        return sum(d * 8**i for i, d in enumerate(order))

    codes = [digits(order) for order in ORDER]
    code = (
        (1 - x) * (1 - c) * codes[0] + (1 - x) * c * codes[1] + x * (1 - c) * codes[2] + x * c * codes[3]
    )

    def step(t, code):
        for i in range(REACH):
            for p in range(4):
                if TAKE[p][i]:
                    @pl.when(jnp.logical_and(t == i, place == p))
                    def _(p=p, i=i):
                        take(TAKE[p][i])
        d = code % 8
        pl.when(d <= me)(lambda: block(d, False))
        return code // 8

    lax.fori_loop(0, REACH, step, code)

    for h in range(heads):
        att[:, h * DV:(h + 1) * DV] = (acc[h, :, :DV] / acc[h, :, DV:]).astype(jnp.bfloat16)
    loads[4].wait()
    width = wout.shape[1]
    tile = 512
    tiles = width // tile

    def store(i):
        at = pl.ds(i * tile, tile)
        return pltpu.make_async_copy(out.at[:, at], o_hbm.at[:, at], out_sem.at[i])

    for i in range(tiles):
        out[:, i * tile:(i + 1) * tile] = jnp.dot(
            att[...], wout[:, i * tile:(i + 1) * tile], preferred_element_type=jnp.float32
        ).astype(jnp.bfloat16)
        store(i).start()
    for i in range(len(sends)):
        @pl.when(sends[i][2])
        def _(i=i):
            for k in range(PARTS):
                remote(i, k).wait_send()
    for i in range(tiles):
        store(i).wait()


def local(n, queries, latent_rope, doc_start, w_kv_up, w_out):
    rows = queries.shape[0]
    heads = w_out.shape[0] // DV
    part = rows // PARTS
    sends = 11
    bf, f32 = jnp.bfloat16, jnp.float32
    return pl.pallas_call(
        functools.partial(kernel, n, heads),
        out_shape=jax.ShapeDtypeStruct((rows, w_out.shape[1]), bf),
        in_specs=[pl.BlockSpec(memory_space=pl.ANY)] * 5,
        out_specs=pl.BlockSpec(memory_space=pl.ANY),
        scratch_shapes=[
            pltpu.VMEM((REACH + 1, PARTS, part + part * DR // R, R), bf),
            pltpu.VMEM(queries.shape, bf),
            pltpu.VMEM((heads, rows, DQ), bf),
            pltpu.VMEM(latent_rope.shape, bf),
            pltpu.VMEM((1, rows), jnp.int32),
            pltpu.VMEM((rows, 128), jnp.int32),
            pltpu.VMEM(w_kv_up.shape, bf),
            pltpu.VMEM(w_out.shape, bf),
            pltpu.VMEM((rows, DR), bf),
            pltpu.VMEM((heads, rows, 2 * DV), f32),
            pltpu.VMEM((heads, rows, 128), f32),
            pltpu.VMEM((rows, heads * DV), bf),
            pltpu.VMEM((rows, w_out.shape[1]), bf),
            pltpu.SemaphoreType.DMA((5,)),
            pltpu.SemaphoreType.DMA((4,)),
            pltpu.SemaphoreType.DMA((sends, PARTS)),
            pltpu.SemaphoreType.DMA((REACH + 1, PARTS)),
        ],
        compiler_params=pltpu.CompilerParams(
            collective_id=0, has_side_effects=True, vmem_limit_bytes=48 * 1024 * 1024
        ),
        cost_estimate=pl.CostEstimate(
            flops=20 * 10**9, bytes_accessed=10**7, transcendentals=8 * heads * rows * rows
        ),
    )(queries, latent_rope, doc_start.reshape(1, rows), w_kv_up, w_out)


def solution(mesh):
    in_specs = (P(("grp", "srv"), None), P(("grp", "srv"), None), P(("grp", "srv")), P(), P())
    out_specs = P(("grp", "srv"), None)
    return jax.shard_map(
        functools.partial(local, mesh.shape["srv"]), mesh=mesh, in_specs=in_specs, out_specs=out_specs,
        check_vma=False,
    )
```

time: 368 us -> 65.1 us (0.18); the launches traced: 362 us -> 64.8 us
  waiting for transfers between devices: 263 us -> 0 us
  Pallas kernels: 0 us -> 58.9 us
  matrix products: 43.6 us -> 0 us
  starting transfers between devices: 39.2 us -> 0 us
  other arithmetic: 8.55 us -> 0 us
    ppermute x14 -> x0, waiting for transfers between devices: 263 us -> none  [passed_along(): lax.ppermute(value, axis, [(source, source + steps) for source in range(i...]
    pallas_call x0 -> x1, Pallas kernels: none -> 58.9 us  [local(): pl.pallas_call(functools.partial(kernel, n, heads), out_shape=jax.ShapeDt...]
    dot_general x26 -> x0, matrix products: 43.6 us -> none  [the longest x8 15.7 us: block_terms(): jnp.einsum('hij,jhc->ihc', weights.astype(jnp.bfloat16), values, preferre...]
    ppermute x14 -> x0, starting transfers between devices: 39.2 us -> none  [passed_along(): lax.ppermute(value, axis, [(source, source + steps) for source in range(i...]
    reduce_sum x8 -> x0, other arithmetic: 7.27 us -> none  [block_terms(): block_total = jnp.sum(weights, axis=2)]
  transfers between devices with their start and end apart: 14 -> 0, of which waited for: 5 -> 0; matrix products, arithmetic and copies ran while one was open for 8% -> 0% of each run, Pallas kernels for 0% -> 0%
where the time goes in v1:
time: 65.1 us; the launch traced here: 64.8 us
  Pallas kernels  58.9 us (90%)
  local copies, waits for them, and re-layouts  5.94 us (9%)
    pallas_call x1, Pallas kernels, local(): pl.pallas_call(functools.partial(kernel, n, heads), out_shape=jax.ShapeDt...  58.9 us
    unnamed x6, local copies, waits for them, and re-layouts  5.26 us

profile of v1, /device:TPU:25, one launch (start us, length us, event | category | flops | bytes accessed | tf_op | source)
XLA Modules:
  0.0 64.8 jit_solution(8159053282852087276)
XLA Ops:
  0.0 0.7 %reshape.3.start_hbm = s32[1,384]{1,0:T(1,128)S(1)} reshape(s32[384]{0:T(512)} %param.7) | data formatting | bytes 3072 | tf_op jit(solution)/shard_map/reshape | solution.py:264
  0.7 1.3 %copy.6.lat_hbm = bf16[384,576]{1,0:T(8,128)(2,1)S(1)} copy(bf16[384,576]{0,1:T(8,128)(2,1)} %param.6) | data formatting | bytes 884736 | tf_op args[1]
  1.9 0.0 copy-start
  2.0 1.6 %copy-done = bf16[512,2048]{1,0:T(8,128)(2,1)S(1)} copy-done((bf16[512,2048]{1,0:T(8,128)(2,1)S(1)}, bf16[512,2048]{1,0:T(8,128)(2,1)}, u32[]{:S(2)}) %copy-start) | copy-done | bytes 2097176
  3.5 0.0 copy-start.1
  3.5 1.3 %copy-done.1 = bf16[384,1536]{1,0:T(8,128)(2,1)S(1)} copy-done((bf16[384,1536]{1,0:T(8,128)(2,1)S(1)}, bf16[384,1536]{1,0:T(8,128)(2,1)}, u32[]{:S(2)}) %copy-start.1) | copy-done | bytes 1179672
  4.8 58.9 %shard_map.55 = bf16[384,2048]{1,0:T(8,128)(2,1)S(1)} custom-call(bf16[384,1536]{1,0:T(8,128)(2,1)S(1)} %copy-done.1, bf16[384,576]{1,0:T(8,128)(2,1)S(1)} %copy.6.lat_hbm, s32[1,384]{1,0:T(1,128)S(1)} %reshape.3.start_hbm, bf16[512,2048]{1,0:T(8,128)(2,1)S(1)} %copy-done, bf16[1024,2048]{1,0:T(8,128)(2,1)} %wout_hbm.1), custom_call_target="tpu_custom_call" | custom-call | flops 20000000000 | bytes 10000000 | tf_op jit(solution)/shard_map/pallas_call | solution.py:234
  63.7 1.1 %copy.8 = bf16[384,2048]{1,0:T(8,128)(2,1)} copy(bf16[384,2048]{1,0:T(8,128)(2,1)S(1)} %shard_map.55) | data formatting | bytes 3145728
Async XLA Ops:
  1.9 1.6 %copy-start = (bf16[512,2048]{1,0:T(8,128)(2,1)S(1)}, bf16[512,2048]{1,0:T(8,128)(2,1)}, u32[]{:S(2)}) copy-start(bf16[512,2048]{1,0:T(8,128)(2,1)} %wkv_hbm.1) | copy-start | bytes 6291460
  3.5 1.3 %copy-start.1 = (bf16[384,1536]{1,0:T(8,128)(2,1)S(1)}, bf16[384,1536]{1,0:T(8,128)(2,1)}, u32[]{:S(2)}) copy-start(bf16[384,1536]{1,0:T(8,128)(2,1)} %q_hbm.1) | copy-start | bytes 3538948

commit v2 on v1

--- a/solution.py
+++ b/solution.py
@@ -15,6 +15,7 @@
 REACH = 7
 DQ = DN + DR
 PARTS = 3
+GROUP = 2
 NEG = -1e30
 MESH = pl.DeviceIdType.MESH
 
@@ -28,24 +29,32 @@
 
 
 def kernel(n, heads, q_hbm, lat_hbm, start_hbm, wkv_hbm, wout_hbm, o_hbm,
-           held, q_in, q_s, lat_in, start_in, start_s, wkv, wout, rope, acc, top, att, out,
-           in_sem, out_sem, send_sem, recv_sem):
+           held, q_in, q_s, start_in, wk, wv, wvt, wout, lat, bias, acc, top, att, out,
+           lat_sem, in_sem, w_sem, out_sem, send_sem, recv_sem):
     rows = q_in.shape[0]
     part = rows // PARTS
-    extra = part * DR // R
     me = lax.axis_index("srv")
     z, x, c = me // 4, (me // 2) % 2, me % 2
     depth = n // 4
     place = 2 * x + c
     scale = math.log2(math.e) / math.sqrt(DQ)
 
+    own_loads = [
+        pltpu.make_async_copy(lat_hbm.at[:, pl.ds(k * part, part)], held.at[0, k], lat_sem.at[k])
+        for k in range(PARTS)
+    ]
     loads = [
         pltpu.make_async_copy(a, b, in_sem.at[i])
-        for i, (a, b) in enumerate(
-            ((lat_hbm, lat_in), (q_hbm, q_in), (start_hbm, start_in), (wkv_hbm, wkv), (wout_hbm, wout))
+        for i, (a, b) in enumerate(((start_hbm, start_in), (q_hbm, q_in), (wout_hbm, wout)))
+    ]
+    w_loads = [
+        pltpu.make_async_copy(
+            wkv_hbm.at[:, pl.ds(h * (DN + DV) + i * DN, DN)], b.at[:, pl.ds(h * DN, DN)], w_sem.at[i, h]
         )
+        for i, b in ((0, wk), (1, wv))
+        for h in range(heads)
     ]
-    for load in loads:
+    for load in own_loads + loads[:2] + w_loads + loads[2:]:
         load.start()
 
     has_next = z + 1 < depth
@@ -114,68 +123,58 @@
     count = count + jnp.logical_and(c == 1, middle).astype(jnp.int32)
     count = count + jnp.logical_and(c == 0, z >= 2).astype(jnp.int32)
 
-    loads[0].wait()
-    for k in range(PARTS):
-        held[0, k, :part, :] = lat_in[k * part:(k + 1) * part, :R]
-        held[0, k, part:, :] = jnp.concatenate(
-            [lat_in[k * part + g * extra:k * part + (g + 1) * extra, R:] for g in range(R // DR)], axis=1
-        )
+    for load in own_loads:
+        load.wait()
     pl.semaphore_wait(barrier, count)
     for k in range(PARTS):
         pass_on(0, k)
 
     loads[1].wait()
     for h in range(heads):
-        q_s[h] = q_in[:, h * DQ:(h + 1) * DQ]
-    loads[2].wait()
-    starts = jnp.broadcast_to(start_in[...].astype(jnp.float32), (128, rows))
-    start_s[...] = jnp.transpose(starts).astype(jnp.int32)
-    loads[3].wait()
+        q_s[h] = jnp.transpose(q_in[:, h * DQ:(h + 1) * DQ])
+    for load in w_loads:
+        load.wait()
+    for h in range(heads):
+        wvt[h * DV:(h + 1) * DV, :] = jnp.transpose(wv[:, h * DV:(h + 1) * DV])
+    loads[0].wait()
 
     def block(d, own):
         for k in range(PARTS):
-            for g in range(R // DR):
-                rope[k * part + g * extra:k * part + (g + 1) * extra, :] = held[
-                    d, k, part:, g * DR:(g + 1) * DR
-                ]
-        first = start_s[...] - (me - d) * rows
-        first = jnp.concatenate([first] * (rows // 128), axis=1)
-        ones = jnp.ones((rows, 128), jnp.bfloat16)
-
-        def one(h):
-            latent = held[d, :, :part, :].reshape(rows, R)
-            columns = pl.ds(pl.multiple_of(h * (DN + DV), DN + DV), DN + DV)
-            kv = jnp.dot(latent, wkv[:, columns], preferred_element_type=jnp.float32).astype(jnp.bfloat16)
-            keys = jnp.concatenate([kv[:, :DN], rope[...]], axis=1)
-            values = jnp.concatenate([kv[:, DN:], ones], axis=1)
-            s = lax.dot_general(
-                q_s[h], keys, (((1,), (1,)), ((), ())), preferred_element_type=jnp.float32
-            )
-            position = lax.broadcasted_iota(jnp.int32, (rows, rows), 1)
-            allowed = position >= first
-            if own:
-                row = lax.broadcasted_iota(jnp.int32, (rows, rows), 0)
-                allowed = jnp.logical_and(allowed, position <= row)
-            s = jnp.where(allowed, s, NEG)
-            best = jnp.max(s, axis=1, keepdims=True)
-            if own:
-                new = jnp.broadcast_to(best, (rows, 128))
-            else:
+            lat[k * part:(k + 1) * part, :] = jnp.transpose(held[d, k])
+        first = start_in[...].reshape(1, rows) - (me - d) * rows
+        position = lax.broadcasted_iota(jnp.int32, (rows, rows), 0)
+        allowed = position >= first
+        if own:
+            allowed = jnp.logical_and(allowed, position <= lax.broadcasted_iota(jnp.int32, (rows, rows), 1))
+        bias[...] = jnp.where(allowed, jnp.float32(0.0), jnp.float32(NEG))
+        ones = jnp.ones((16, rows), jnp.bfloat16)
+
+        def one(h, k_nope, values):
+            keys = jnp.concatenate([k_nope, lat[:, R:]], axis=1)
+            s = jnp.dot(keys, q_s[h], preferred_element_type=jnp.float32) + bias[...]
+            new = jnp.max(s, axis=0, keepdims=True)
+            if not own:
                 old = top[h]
-                new = jnp.maximum(old, best)
-            p = jnp.exp2((s - jnp.concatenate([new] * (rows // 128), axis=1)) * scale)
-            pv = jnp.dot(p.astype(jnp.bfloat16), values, preferred_element_type=jnp.float32)
+                new = jnp.maximum(old, new)
+            p = jnp.exp2((s - new) * scale)
+            values = jnp.concatenate([values, ones], axis=0)
+            pv = jnp.dot(values, p.astype(jnp.bfloat16), preferred_element_type=jnp.float32)
             if own:
                 acc[h] = pv
             else:
-                factor = jnp.exp2((old - new) * scale)
-                acc[h] = acc[h] * jnp.concatenate([factor, factor], axis=1) + pv
+                acc[h] = acc[h] * jnp.exp2((old - new) * scale) + pv
             top[h] = new
 
-        @pl.loop(0, heads // 2)
-        def _(pair):
-            one(2 * pair)
-            one(2 * pair + 1)
+        @pl.loop(0, heads // GROUP)
+        def _(group):
+            at = pl.ds(pl.multiple_of(group * GROUP * DN, GROUP * DN), GROUP * DN)
+            latent_t = jnp.concatenate([held[d, k, :R, :] for k in range(PARTS)], axis=1)
+            k_nope = jnp.dot(lat[:, :R], wk[:, at], preferred_element_type=jnp.float32)
+            k_nope = k_nope.astype(jnp.bfloat16)
+            values = jnp.dot(wvt[at, :], latent_t, preferred_element_type=jnp.float32)
+            values = values.astype(jnp.bfloat16)
+            for i in range(GROUP):
+                one(group * GROUP + i, k_nope[:, i * DN:(i + 1) * DN], values[i * DV:(i + 1) * DV, :])
 
     block(0, True)
 
@@ -201,8 +200,9 @@
     lax.fori_loop(0, REACH, step, code)
 
     for h in range(heads):
-        att[:, h * DV:(h + 1) * DV] = (acc[h, :, :DV] / acc[h, :, DV:]).astype(jnp.bfloat16)
-    loads[4].wait()
+        attended = acc[h, :DV, :] / acc[h, DV:DV + 1, :]
+        att[:, h * DV:(h + 1) * DV] = jnp.transpose(attended.astype(jnp.bfloat16))
+    loads[2].wait()
     width = wout.shape[1]
     tile = 512
     tiles = width // tile
@@ -234,23 +234,26 @@
     return pl.pallas_call(
         functools.partial(kernel, n, heads),
         out_shape=jax.ShapeDtypeStruct((rows, w_out.shape[1]), bf),
-        in_specs=[pl.BlockSpec(memory_space=pl.ANY)] * 5,
-        out_specs=pl.BlockSpec(memory_space=pl.ANY),
+        in_specs=[pl.BlockSpec(memory_space=pltpu.HBM)] * 5,
+        out_specs=pl.BlockSpec(memory_space=pltpu.HBM),
         scratch_shapes=[
-            pltpu.VMEM((REACH + 1, PARTS, part + part * DR // R, R), bf),
+            pltpu.VMEM((REACH + 1, PARTS, R + DR, part), bf),
             pltpu.VMEM(queries.shape, bf),
-            pltpu.VMEM((heads, rows, DQ), bf),
+            pltpu.VMEM((heads, DQ, rows), bf),
+            pltpu.VMEM(doc_start.shape, jnp.int32),
+            pltpu.VMEM((R, heads * DN), bf),
+            pltpu.VMEM((R, heads * DV), bf),
+            pltpu.VMEM((heads * DV, R), bf),
+            pltpu.VMEM(w_out.shape, bf),
             pltpu.VMEM(latent_rope.shape, bf),
-            pltpu.VMEM((1, rows), jnp.int32),
-            pltpu.VMEM((rows, 128), jnp.int32),
-            pltpu.VMEM(w_kv_up.shape, bf),
-            pltpu.VMEM(w_out.shape, bf),
-            pltpu.VMEM((rows, DR), bf),
-            pltpu.VMEM((heads, rows, 2 * DV), f32),
-            pltpu.VMEM((heads, rows, 128), f32),
+            pltpu.VMEM((rows, rows), f32),
+            pltpu.VMEM((heads, DV + 16, rows), f32),
+            pltpu.VMEM((heads, 1, rows), f32),
             pltpu.VMEM((rows, heads * DV), bf),
             pltpu.VMEM((rows, w_out.shape[1]), bf),
-            pltpu.SemaphoreType.DMA((5,)),
+            pltpu.SemaphoreType.DMA((PARTS,)),
+            pltpu.SemaphoreType.DMA((3,)),
+            pltpu.SemaphoreType.DMA((2, heads)),
             pltpu.SemaphoreType.DMA((4,)),
             pltpu.SemaphoreType.DMA((sends, PARTS)),
             pltpu.SemaphoreType.DMA((REACH + 1, PARTS)),
@@ -261,7 +264,7 @@
         cost_estimate=pl.CostEstimate(
             flops=20 * 10**9, bytes_accessed=10**7, transcendentals=8 * heads * rows * rows
         ),
-    )(queries, latent_rope, doc_start.reshape(1, rows), w_kv_up, w_out)
+    )(queries, latent_rope.T, doc_start, w_kv_up, w_out)
 
 
 def solution(mesh):

time: 65.1 us -> 65.5 us (level)
  Pallas kernels: 58.9 us -> 59.6 us
    pallas_call x1, Pallas kernels: 58.9 us -> 59.6 us  [local(): pl.pallas_call(functools.partial(kernel, n, heads), out_shape=jax.ShapeDt...]
    reshape x1 -> x0, local copies, waits for them, and re-layouts: 0.68 us -> none  [local(): doc_start.reshape(1, rows)]
    unnamed x6 -> x9, local copies, waits for them, and re-layouts: 5.26 us -> 5.7 us
where the time goes in v2:
time: 65.5 us; the launch traced here: 65.3 us
  Pallas kernels  59.6 us (91%)
  local copies, waits for them, and re-layouts  5.7 us (9%)
    pallas_call x1, Pallas kernels, local(): pl.pallas_call(functools.partial(kernel, n, heads), out_shape=jax.ShapeDt...  59.6 us
    unnamed x9, local copies, waits for them, and re-layouts  5.7 us

profile of v2, /device:TPU:25, one launch (start us, length us, event | category | flops | bytes accessed | tf_op | source)
XLA Modules:
  0.0 65.3 jit_solution(5722429747695565667)
XLA Ops:
  0.0 0.0 copy-start
  0.0 1.6 %copy-done = bf16[512,2048]{1,0:T(8,128)(2,1)S(1)} copy-done((bf16[512,2048]{1,0:T(8,128)(2,1)S(1)}, bf16[512,2048]{1,0:T(8,128)(2,1)}, u32[]{:S(2)}) %copy-start) | copy-done | bytes 2097176
  1.6 0.0 copy-start.1
  1.6 1.3 %copy-done.1 = bf16[384,1536]{1,0:T(8,128)(2,1)S(1)} copy-done((bf16[384,1536]{1,0:T(8,128)(2,1)S(1)}, bf16[384,1536]{1,0:T(8,128)(2,1)}, u32[]{:S(2)}) %copy-start.1) | copy-done | bytes 1179672
  2.9 0.0 copy-start.2
  2.9 1.0 %copy-done.2 = bf16[384,576]{0,1:T(8,128)(2,1)S(1)} copy-done((bf16[384,576]{0,1:T(8,128)(2,1)S(1)}, bf16[384,576]{0,1:T(8,128)(2,1)}, u32[]{:S(2)}) %copy-start.2) | copy-done | bytes 442392
  3.9 0.0 copy-start.3
  3.9 0.7 %copy-done.3 = s32[384]{0:T(512)S(1)} copy-done((s32[384]{0:T(512)S(1)}, s32[384]{0:T(512)}, u32[]{:S(2)}) %copy-start.3) | copy-done | bytes 1560
  4.6 59.6 %shard_map.55 = bf16[384,2048]{1,0:T(8,128)(2,1)S(1)} custom-call(bf16[384,1536]{1,0:T(8,128)(2,1)S(1)} %copy-done.1, bf16[576,384]{1,0:T(8,128)(2,1)S(1)} %bitcast.1, s32[384]{0:T(512)S(1)} %copy-done.3, bf16[512,2048]{1,0:T(8,128)(2,1)S(1)} %copy-done, bf16[1024,2048]{1,0:T(8,128)(2,1)} %wout_hbm.1), custom_call_target="tpu_custom_call" | custom-call | flops 20000000000 | bytes 10000000 | tf_op jit(solution)/shard_map/pallas_call | solution.py:234
  64.1 1.1 %copy.7 = bf16[384,2048]{1,0:T(8,128)(2,1)} copy(bf16[384,2048]{1,0:T(8,128)(2,1)S(1)} %shard_map.55) | data formatting | bytes 3145728
Async XLA Ops:
  0.0 1.6 %copy-start = (bf16[512,2048]{1,0:T(8,128)(2,1)S(1)}, bf16[512,2048]{1,0:T(8,128)(2,1)}, u32[]{:S(2)}) copy-start(bf16[512,2048]{1,0:T(8,128)(2,1)} %wkv_hbm.1) | copy-start | bytes 6291460
  1.6 1.3 %copy-start.1 = (bf16[384,1536]{1,0:T(8,128)(2,1)S(1)}, bf16[384,1536]{1,0:T(8,128)(2,1)}, u32[]{:S(2)}) copy-start(bf16[384,1536]{1,0:T(8,128)(2,1)} %q_hbm.1) | copy-start | bytes 3538948
  2.9 1.0 %copy-start.2 = (bf16[384,576]{0,1:T(8,128)(2,1)S(1)}, bf16[384,576]{0,1:T(8,128)(2,1)}, u32[]{:S(2)}) copy-start(bf16[384,576]{0,1:T(8,128)(2,1)} %param.6) | copy-start | bytes 1327108
  3.9 0.7 %copy-start.3 = (s32[384]{0:T(512)S(1)}, s32[384]{0:T(512)}, u32[]{:S(2)}) copy-start(s32[384]{0:T(512)} %start_hbm.1) | copy-start | bytes 4612

commit v3 on v2

--- a/solution.py
+++ b/solution.py
@@ -15,7 +15,6 @@
 REACH = 7
 DQ = DN + DR
 PARTS = 3
-GROUP = 2
 NEG = -1e30
 MESH = pl.DeviceIdType.MESH
 
@@ -149,32 +148,44 @@
         bias[...] = jnp.where(allowed, jnp.float32(0.0), jnp.float32(NEG))
         ones = jnp.ones((16, rows), jnp.bfloat16)
 
-        def one(h, k_nope, values):
-            keys = jnp.concatenate([k_nope, lat[:, R:]], axis=1)
-            s = jnp.dot(keys, q_s[h], preferred_element_type=jnp.float32) + bias[...]
+        latent_t = jnp.concatenate([held[d, k, :R, :] for k in range(PARTS)], axis=1)
+
+        def expand(pair):
+            at = slice(pair * 2 * DN, (pair + 1) * 2 * DN)
+            k_nope = jnp.dot(lat[:, :R], wk[:, at], preferred_element_type=jnp.float32)
+            values = jnp.dot(wvt[at, :], latent_t, preferred_element_type=jnp.float32)
+            return k_nope.astype(jnp.bfloat16), values.astype(jnp.bfloat16)
+
+        def score(h, pair):
+            i = h % 2
+            keys = jnp.concatenate([pair[0][:, i * DN:(i + 1) * DN], lat[:, R:]], axis=1)
+            return jnp.dot(keys, q_s[h], preferred_element_type=jnp.float32)
+
+        def weigh(h, s):
+            s = s + bias[...]
             new = jnp.max(s, axis=0, keepdims=True)
+            factor = None
             if not own:
                 old = top[h]
                 new = jnp.maximum(old, new)
-            p = jnp.exp2((s - new) * scale)
-            values = jnp.concatenate([values, ones], axis=0)
-            pv = jnp.dot(values, p.astype(jnp.bfloat16), preferred_element_type=jnp.float32)
-            if own:
-                acc[h] = pv
-            else:
-                acc[h] = acc[h] * jnp.exp2((old - new) * scale) + pv
+                factor = jnp.exp2((old - new) * scale)
             top[h] = new
-
-        @pl.loop(0, heads // GROUP)
-        def _(group):
-            at = pl.ds(pl.multiple_of(group * GROUP * DN, GROUP * DN), GROUP * DN)
-            latent_t = jnp.concatenate([held[d, k, :R, :] for k in range(PARTS)], axis=1)
-            k_nope = jnp.dot(lat[:, :R], wk[:, at], preferred_element_type=jnp.float32)
-            k_nope = k_nope.astype(jnp.bfloat16)
-            values = jnp.dot(wvt[at, :], latent_t, preferred_element_type=jnp.float32)
-            values = values.astype(jnp.bfloat16)
-            for i in range(GROUP):
-                one(group * GROUP + i, k_nope[:, i * DN:(i + 1) * DN], values[i * DV:(i + 1) * DV, :])
+            return jnp.exp2((s - new) * scale).astype(jnp.bfloat16), factor
+
+        def add(h, pair, p, factor):
+            i = h % 2
+            values = jnp.concatenate([pair[1][i * DV:(i + 1) * DV, :], ones], axis=0)
+            pv = jnp.dot(values, p, preferred_element_type=jnp.float32)
+            acc[h] = pv if own else acc[h] * factor + pv
+
+        pairs = {0: expand(0)}
+        scores = {0: score(0, pairs[0])}
+        for h in range(heads):
+            if h + 1 < heads:
+                scores[h + 1] = score(h + 1, pairs[(h + 1) // 2])
+            if h % 2 == 0 and h + 2 < heads:
+                pairs[h // 2 + 1] = expand(h // 2 + 1)
+            add(h, pairs[h // 2], *weigh(h, scores.pop(h)))
 
     block(0, True)
 
@@ -259,7 +270,7 @@
             pltpu.SemaphoreType.DMA((REACH + 1, PARTS)),
         ],
         compiler_params=pltpu.CompilerParams(
-            collective_id=0, has_side_effects=True, vmem_limit_bytes=48 * 1024 * 1024
+            collective_id=0, has_side_effects=True, vmem_limit_bytes=60 * 1024 * 1024
         ),
         cost_estimate=pl.CostEstimate(
             flops=20 * 10**9, bytes_accessed=10**7, transcendentals=8 * heads * rows * rows

time: 65.5 us -> 55.1 us (0.84)
  Pallas kernels: 59.6 us -> 52.3 us
  local copies, waits for them, and re-layouts: 5.7 us -> 2.73 us
    pallas_call x1, Pallas kernels: 59.6 us -> 52.3 us  [local(): pl.pallas_call(functools.partial(kernel, n, heads), out_shape=jax.ShapeDt...]
    unnamed x9 -> x1, local copies, waits for them, and re-layouts: 5.7 us -> 2.73 us
where the time goes in v3:
time: 55.1 us; the launch traced here: 55 us
  Pallas kernels  52.3 us (95%)
  local copies, waits for them, and re-layouts  2.73 us (5%)
    pallas_call x1, Pallas kernels, local(): pl.pallas_call(functools.partial(kernel, n, heads), out_shape=jax.ShapeDt...  52.3 us
    unnamed x1, local copies, waits for them, and re-layouts  2.73 us

profile of v3, /device:TPU:25, one launch (start us, length us, event | category | flops | bytes accessed | tf_op | source)
XLA Modules:
  0.0 55.0 jit_solution(10341473865464559976)
XLA Ops:
  0.0 52.3 %shard_map.55 = bf16[384,2048]{1,0:T(8,128)(2,1)} custom-call(bf16[384,1536]{1,0:T(8,128)(2,1)} %q_hbm.1, bf16[576,384]{1,0:T(8,128)(2,1)} %bitcast.1, s32[384]{0:T(512)} %start_hbm.1, bf16[512,2048]{1,0:T(8,128)(2,1)} %wkv_hbm.1, bf16[1024,2048]{1,0:T(8,128)(2,1)} %wout_hbm.1), custom_call_target="tpu_custom_call" | custom-call | flops 20000000000 | bytes 10000000 | tf_op jit(solution)/shard_map/pallas_call | solution.py:245
  52.3 2.7 %copy.7 = bf16[384,2048]{1,0:T(8,128)(2,1)} copy(bf16[384,2048]{1,0:T(8,128)(2,1)} %shard_map.55) | data formatting | bytes 3145728

commit v4 on v3

--- a/solution.py
+++ b/solution.py
@@ -18,17 +18,17 @@
 NEG = -1e30
 MESH = pl.DeviceIdType.MESH
 
-ORDER = ((4, 3, 7, 2, 1, 5, 6), (1, 4, 5, 2, 3, 6, 7), (2, 1, 4, 3, 7, 6, 5), (1, 2, 3, 4, 5, 6, 7))
+ORDER = ((4, 2, 3, 6, 1, 7, 5), (1, 5, 4, 3, 2, 7, 6), (2, 4, 1, 3, 6, 7, 5), (1, 3, 2, 4, 5, 7, 6))
 TAKE = (
-    ((4,), (3,), (7,), (2,), (1,), (5,), (6,)),
-    ((1,), (4,), (5,), (2,), (3,), (6,), (7,)),
-    ((2, 4), (1,), (), (3, 7), (6,), (), (5,)),
-    ((1,), (2, 4), (3,), (), (6, 5), (), (7,)),
+    ((4,), (2,), (3,), (6,), (1,), (7, 5), ()),
+    ((1,), (5,), (4,), (3,), (2,), (7,), (6,)),
+    ((2, 4), (), (1, 6), (3, 7), (), (), (5,)),
+    ((1,), (3, 2, 4), (), (), (5, 6), (7,), ()),
 )
 
 
-def kernel(n, heads, q_hbm, lat_hbm, start_hbm, wkv_hbm, wout_hbm, o_hbm,
-           held, q_in, q_s, start_in, wk, wv, wvt, wout, lat, bias, acc, top, att, out,
+def kernel(n, heads, q_hbm, lat_hbm, start_hbm, wkv_hbm, o_hbm,
+           held, q_in, q_s, start_in, wk, wv, wvt, lat, bias, acc, top, att,
            lat_sem, in_sem, w_sem, out_sem, send_sem, recv_sem):
     rows = q_in.shape[0]
     part = rows // PARTS
@@ -44,7 +44,7 @@
     ]
     loads = [
         pltpu.make_async_copy(a, b, in_sem.at[i])
-        for i, (a, b) in enumerate(((start_hbm, start_in), (q_hbm, q_in), (wout_hbm, wout)))
+        for i, (a, b) in enumerate(((start_hbm, start_in), (q_hbm, q_in)))
     ]
     w_loads = [
         pltpu.make_async_copy(
@@ -53,7 +53,7 @@
         for i, b in ((0, wk), (1, wv))
         for h in range(heads)
     ]
-    for load in own_loads + loads[:2] + w_loads + loads[2:]:
+    for load in own_loads + loads + w_loads:
         load.start()
 
     has_next = z + 1 < depth
@@ -125,8 +125,10 @@
     for load in own_loads:
         load.wait()
     pl.semaphore_wait(barrier, count)
-    for k in range(PARTS):
-        pass_on(0, k)
+    @pl.when(c == 0)
+    def _():
+        for k in range(PARTS):
+            pass_on(0, k)
 
     loads[1].wait()
     for h in range(heads):
@@ -189,6 +191,11 @@
 
     block(0, True)
 
+    @pl.when(c == 1)
+    def _():
+        for k in range(PARTS):
+            pass_on(0, k)
+
     def digits(order):
         return sum(d * 8**i for i, d in enumerate(order))
 
@@ -213,27 +220,14 @@
     for h in range(heads):
         attended = acc[h, :DV, :] / acc[h, DV:DV + 1, :]
         att[:, h * DV:(h + 1) * DV] = jnp.transpose(attended.astype(jnp.bfloat16))
-    loads[2].wait()
-    width = wout.shape[1]
-    tile = 512
-    tiles = width // tile
-
-    def store(i):
-        at = pl.ds(i * tile, tile)
-        return pltpu.make_async_copy(out.at[:, at], o_hbm.at[:, at], out_sem.at[i])
-
-    for i in range(tiles):
-        out[:, i * tile:(i + 1) * tile] = jnp.dot(
-            att[...], wout[:, i * tile:(i + 1) * tile], preferred_element_type=jnp.float32
-        ).astype(jnp.bfloat16)
-        store(i).start()
+    store = pltpu.make_async_copy(att, o_hbm, out_sem)
+    store.start()
     for i in range(len(sends)):
         @pl.when(sends[i][2])
         def _(i=i):
             for k in range(PARTS):
                 remote(i, k).wait_send()
-    for i in range(tiles):
-        store(i).wait()
+    store.wait()
 
 
 def local(n, queries, latent_rope, doc_start, w_kv_up, w_out):
@@ -242,10 +236,10 @@
     part = rows // PARTS
     sends = 11
     bf, f32 = jnp.bfloat16, jnp.float32
-    return pl.pallas_call(
+    attended = pl.pallas_call(
         functools.partial(kernel, n, heads),
-        out_shape=jax.ShapeDtypeStruct((rows, w_out.shape[1]), bf),
-        in_specs=[pl.BlockSpec(memory_space=pltpu.HBM)] * 5,
+        out_shape=jax.ShapeDtypeStruct((rows, heads * DV), bf),
+        in_specs=[pl.BlockSpec(memory_space=pltpu.HBM)] * 4,
         out_specs=pl.BlockSpec(memory_space=pltpu.HBM),
         scratch_shapes=[
             pltpu.VMEM((REACH + 1, PARTS, R + DR, part), bf),
@@ -255,17 +249,15 @@
             pltpu.VMEM((R, heads * DN), bf),
             pltpu.VMEM((R, heads * DV), bf),
             pltpu.VMEM((heads * DV, R), bf),
-            pltpu.VMEM(w_out.shape, bf),
             pltpu.VMEM(latent_rope.shape, bf),
             pltpu.VMEM((rows, rows), f32),
             pltpu.VMEM((heads, DV + 16, rows), f32),
             pltpu.VMEM((heads, 1, rows), f32),
             pltpu.VMEM((rows, heads * DV), bf),
-            pltpu.VMEM((rows, w_out.shape[1]), bf),
             pltpu.SemaphoreType.DMA((PARTS,)),
-            pltpu.SemaphoreType.DMA((3,)),
+            pltpu.SemaphoreType.DMA((2,)),
             pltpu.SemaphoreType.DMA((2, heads)),
-            pltpu.SemaphoreType.DMA((4,)),
+            pltpu.SemaphoreType.DMA,
             pltpu.SemaphoreType.DMA((sends, PARTS)),
             pltpu.SemaphoreType.DMA((REACH + 1, PARTS)),
         ],
@@ -275,7 +267,8 @@
         cost_estimate=pl.CostEstimate(
             flops=20 * 10**9, bytes_accessed=10**7, transcendentals=8 * heads * rows * rows
         ),
-    )(queries, latent_rope.T, doc_start, w_kv_up, w_out)
+    )(queries, latent_rope.T, doc_start, w_kv_up)
+    return jnp.dot(attended, w_out, preferred_element_type=f32).astype(bf)
 
 
 def solution(mesh):

time: 55.1 us -> 54 us (0.980)
  the two profiles are of different devices: /device:TPU:25 before, /device:TPU:15 now
where the time goes in v4:
time: 54 us; the launch traced here: 53.8 us
  Pallas kernels  48.4 us (90%)
  matrix products  5.37 us (10%)
    pallas_call x1, Pallas kernels, local(): pl.pallas_call(functools.partial(kernel, n, heads), out_shape=jax.ShapeDt...  48.4 us
    dot_general x1, matrix products, local(): return jnp.dot(attended, w_out, preferred_element_type=f32).astype(bf)  5.37 us

profile of v4, /device:TPU:15, one launch (start us, length us, event | category | flops | bytes accessed | tf_op | source)
XLA Modules:
  0.0 53.8 jit_solution(1126067912451556194)
XLA Ops:
  0.0 48.4 %shard_map.55 = bf16[384,1024]{1,0:T(8,128)(2,1)} custom-call(bf16[384,1536]{1,0:T(8,128)(2,1)} %q_hbm.1, bf16[576,384]{1,0:T(8,128)(2,1)} %bitcast.3, s32[384]{0:T(512)} %start_hbm.1, bf16[512,2048]{1,0:T(8,128)(2,1)} %wkv_hbm.1), custom_call_target="tpu_custom_call" | custom-call | flops 20000000000 | bytes 10000000 | tf_op jit(solution)/shard_map/pallas_call | solution.py:239
  48.5 5.4 %convolution_convert_fusion = bf16[384,2048]{1,0:T(8,128)(2,1)} fusion(bf16[384,1024]{1,0:T(8,128)(2,1)} %shard_map.55, bf16[1024,2048]{1,0:T(8,128)(2,1)} %param.9), kind=kOutput, calls=%fused_computation | convolution fusion | flops 1611399168 | bytes 6553600 | tf_op jit(solution)/shard_map/dot_general | solution.py:271

commit v5 on v3

--- a/solution.py
+++ b/solution.py
@@ -18,12 +18,12 @@
 NEG = -1e30
 MESH = pl.DeviceIdType.MESH
 
-ORDER = ((4, 3, 7, 2, 1, 5, 6), (1, 4, 5, 2, 3, 6, 7), (2, 1, 4, 3, 7, 6, 5), (1, 2, 3, 4, 5, 6, 7))
+ORDER = ((4, 2, 3, 6, 1, 7, 5), (1, 5, 3, 4, 2, 7, 6), (2, 4, 1, 6, 3, 7, 5), (1, 3, 2, 4, 5, 7, 6))
 TAKE = (
-    ((4,), (3,), (7,), (2,), (1,), (5,), (6,)),
-    ((1,), (4,), (5,), (2,), (3,), (6,), (7,)),
-    ((2, 4), (1,), (), (3, 7), (6,), (), (5,)),
-    ((1,), (2, 4), (3,), (), (6, 5), (), (7,)),
+    ((4,), (2,), (3,), (6,), (1,), (7, 5), ()),
+    ((1,), (5,), (3, 4), (2,), (), (7,), (6,)),
+    ((2, 4), (), (1, 6), (3,), (7,), (), (5,)),
+    ((1,), (3, 2), (4,), (5,), (6,), (7,), ()),
 )
 
 
@@ -125,8 +125,10 @@
     for load in own_loads:
         load.wait()
     pl.semaphore_wait(barrier, count)
-    for k in range(PARTS):
-        pass_on(0, k)
+    @pl.when(c == 0)
+    def _():
+        for k in range(PARTS):
+            pass_on(0, k)
 
     loads[1].wait()
     for h in range(heads):
@@ -188,6 +190,11 @@
             add(h, pairs[h // 2], *weigh(h, scores.pop(h)))
 
     block(0, True)
+
+    @pl.when(c == 1)
+    def _():
+        for k in range(PARTS):
+            pass_on(0, k)
 
     def digits(order):
         return sum(d * 8**i for i, d in enumerate(order))
@@ -270,7 +277,7 @@
             pltpu.SemaphoreType.DMA((REACH + 1, PARTS)),
         ],
         compiler_params=pltpu.CompilerParams(
-            collective_id=0, has_side_effects=True, vmem_limit_bytes=60 * 1024 * 1024
+            collective_id=0, has_side_effects=True, vmem_limit_bytes=58 * 1024 * 1024
         ),
         cost_estimate=pl.CostEstimate(
             flops=20 * 10**9, bytes_accessed=10**7, transcendentals=8 * heads * rows * rows

time: 55.1 us -> 55.4 us (level)
  no operation moved by 1% of the time
where the time goes in v5:
time: 55.4 us; the launch traced here: 55.2 us
  Pallas kernels  52.5 us (95%)
  local copies, waits for them, and re-layouts  2.73 us (5%)
    pallas_call x1, Pallas kernels, local(): pl.pallas_call(functools.partial(kernel, n, heads), out_shape=jax.ShapeDt...  52.5 us
    unnamed x1, local copies, waits for them, and re-layouts  2.73 us

profile of v5, /device:TPU:25, one launch (start us, length us, event | category | flops | bytes accessed | tf_op | source)
XLA Modules:
  0.0 55.2 jit_solution(13206533680937516868)
XLA Ops:
  0.0 52.5 %shard_map.55 = bf16[384,2048]{1,0:T(8,128)(2,1)} custom-call(bf16[384,1536]{1,0:T(8,128)(2,1)} %q_hbm.1, bf16[576,384]{1,0:T(8,128)(2,1)} %bitcast.1, s32[384]{0:T(512)} %start_hbm.1, bf16[512,2048]{1,0:T(8,128)(2,1)} %wkv_hbm.1, bf16[1024,2048]{1,0:T(8,128)(2,1)} %wout_hbm.1), custom_call_target="tpu_custom_call" | custom-call | flops 20000000000 | bytes 10000000 | tf_op jit(solution)/shard_map/pallas_call | solution.py:252
  52.5 2.7 %copy.7 = bf16[384,2048]{1,0:T(8,128)(2,1)} copy(bf16[384,2048]{1,0:T(8,128)(2,1)} %shard_map.55) | data formatting | bytes 3145728
